TPU v7x, 256 devices: a whole 4x4x8 slice. The times are simulated.
256 devices in a mesh: space: 32 (over y, z_hi, core), tm: 8 (over z_lo, x).
Axes of the slice: x: 4, y: 4, z: 8 (z_hi: 4, z_lo: 2; z = z_hi * 2 + z_lo), core: 2. Of those that a mesh axis runs over, the one named last changes fastest.
Arguments:
- activity: bfloat16 [2048, 256, 512], P('space', 'tm'), may hold values from 0 to 8
- footprints: bfloat16 [32, 8, 16, 4, 512], P('space'), may hold values from 0.0099487305 to 1
- traces: float32 [32, 8, 16, 256], P('space', None, None, 'tm'), may hold values from 0.1 to 2
- bg_space: float32 [2, 2048, 512], P(None, 'space'), may hold values from 0.05 to 14, as said below
- bg_time: float32 [2, 256], P(None, 'tm'), may hold values from 0.5 to 2
- block_lists: int32 [32, 8, 4], P('space'), may hold values from 0 to 71, as said below
- group_order: int32 [32, 8], P('space'), may hold values from 0 to 7, each once within a row
Outputs:
- traces_out: float32 [32, 8, 16, 256], P('space', None, None, 'tm')
- footprints_out: bfloat16 [32, 8, 16, 4, 512], P('space')
- bg_space_out: float32 [2, 2048, 512], P(None, 'space')
- bg_time_out: float32 [2, 256], P(None, 'tm')
Inputs may be any that keep to these rules, and one draw needn't show every extreme that they name: `block_lists`: the 4 entries of a group differ. Entries below 4 or from 68 on lie in a neighbouring tile; a group has at most one of them, never one outside the grid, and each such entry of a tile with both neighbours is held by exactly one of its groups. `group_order`: each tile's row holds every group number once. `bg_space`: Positive.
All inputs are finite; a program needn't handle non-finite values.
Results may differ from a plain program's by a relative error of at most 0.014.
The roundings to bfloat16 on the way count: a program that leaves them out, or rounds other values in their place, can miss the bound.
Values may be sent and summed in bfloat16 or wider, within the bound.
A program may use at most 128 MiB of HBM per device.

v0:
```python
import jax
import jax.numpy as jnp
from jax import lax
from jax.sharding import PartitionSpec as P

NG_DEV = 8
BPG = 4
BV = 512
VB = 64
ROUNDS = 2
HB = 4


ridge_trace = 0.01
ridge_foot = 0.1


def with_halo(block, sides, width):
    for axis, dim in sides:
        count = lax.axis_size(axis)
        forward = [(i, i + 1) for i in range(count - 1)]
        backward = [(target, source) for source, target in forward]
        low = lax.ppermute(
            lax.slice_in_dim(block, block.shape[dim] - width, None, axis=dim), axis, forward
        )
        high = lax.ppermute(lax.slice_in_dim(block, 0, width, axis=dim), axis, backward)
        block = jnp.concatenate([low, block, high], axis=dim)
    return block


def group_inverse(matrices):
    lower_factor = jnp.linalg.cholesky(matrices)
    identity = jnp.broadcast_to(jnp.eye(matrices.shape[-1], dtype=matrices.dtype), matrices.shape)
    inverse_low = lax.linalg.triangular_solve(lower_factor, identity, left_side=True, lower=True)
    return jnp.einsum("gji,gjk->gik", inverse_low, inverse_low, precision=lax.Precision.HIGHEST)


def tile_gram(footprint, block_row):
    flattened = footprint.reshape(-1, footprint.shape[-1])
    paired = jnp.dot(flattened, flattened.T, preferred_element_type=jnp.float32)
    groups, members, extent = (footprint.shape[0], footprint.shape[1], footprint.shape[2])
    paired = paired.reshape(groups, members, extent, groups, members, extent)
    shared = (block_row[:, :, None, None] == block_row[None, None, :, :]).astype(jnp.float32)
    return jnp.sum(paired * shared[:, None, :, :, None, :], axis=(2, 5))


def residual(footprint, trace_low, bg_space, bg_time, activity, selector):
    frames = activity.shape[1]
    contrib = jnp.einsum("gnkv,gnt->gktv", footprint, trace_low, preferred_element_type=jnp.float32)
    flat_rows = contrib.reshape(-1, frames * BV)
    rebuilt = jnp.einsum("re,rx->ex", selector, flat_rows, precision=lax.Precision.HIGHEST).reshape(
        -1, frames, BV
    )
    middle = rebuilt[HB : HB + VB]
    trace_near = None
    spilled = jnp.concatenate([rebuilt[:HB], rebuilt[HB + VB :]], 0)
    arrived = with_halo(spilled, (("space", 0),), HB)
    middle = middle.at[:HB].add(arrived[:HB]).at[VB - HB :].add(arrived[3 * HB :])
    backdrop = jnp.einsum("cbv,ct->btv", bg_space, bg_time, precision=lax.Precision.HIGHEST)
    residue = (activity.astype(jnp.float32) - middle - backdrop).astype(jnp.bfloat16)
    extended_res = with_halo(residue, (("space", 0),), HB)
    return (residue, extended_res, trace_near)


def pieces_of(extended_res, block_row):
    return jnp.take(extended_res, block_row.reshape(-1), axis=0).reshape(
        NG_DEV, BPG, extended_res.shape[1], BV
    )


def temporal(footprint, traces_now, drives, block_row, order_row):
    gram_matrix = tile_gram(footprint, block_row)
    members = footprint.shape[1]
    picks = jnp.arange(NG_DEV)
    diagonal = gram_matrix[picks, :, picks, :]
    inverse = group_inverse(diagonal + ridge_trace * BPG * BV * jnp.eye(members, dtype=jnp.float32))
    current = traces_now
    for position in range(NG_DEV):
        chosen = order_row[position]
        coupling = gram_matrix[chosen].reshape(members, -1)
        change = (current - traces_now).reshape(-1, current.shape[-1])
        remain = drives[chosen] - jnp.dot(coupling, change, precision=lax.Precision.HIGHEST)
        updated = jnp.maximum(
            current[chosen] + jnp.dot(inverse[chosen], remain, precision=lax.Precision.HIGHEST), 0.0
        )
        current = current.at[chosen].set(updated)
    return current


def body(activity, footprints, traces, bg_space, bg_time, block_lists, group_order):
    footprint = footprints[0]
    traces_now = traces[0]
    block_row = block_lists[0]
    order_row = group_order[0]
    extent = VB + 2 * HB
    selector = (
        block_row.reshape(-1)[:, None] == jnp.arange(extent, dtype=jnp.int32)[None, :]
    ).astype(jnp.float32)
    members = footprint.shape[1]
    eye_small = jnp.eye(members, dtype=jnp.float32)
    all_frames = traces_now.shape[-1] * lax.axis_size("tm")
    for round_id in range(ROUNDS):
        trace_low = traces_now.astype(jnp.bfloat16)
        residue, extended_res, trace_near = residual(
            footprint, trace_low, bg_space, bg_time, activity, selector
        )
        pieces = pieces_of(extended_res, block_row)
        drives = jnp.einsum("gnkv,gktv->gnt", footprint, pieces, preferred_element_type=jnp.float32)
        traces_now = temporal(footprint, traces_now, drives, block_row, order_row)
        trace_low = traces_now.astype(jnp.bfloat16)
        residue, extended_res, trace_near = residual(
            footprint, trace_low, bg_space, bg_time, activity, selector
        )
        observed = residue.astype(jnp.float32)
        voxel_part = jnp.einsum("cbv,btv->ct", bg_space, observed, precision=lax.Precision.HIGHEST)
        squares_space_part = jnp.sum(bg_space * bg_space, axis=(1, 2))
        voxel_sum, squares_space = lax.psum((voxel_part, squares_space_part), "space")
        frame_part = jnp.einsum("btv,ct->cbv", observed, bg_time, precision=lax.Precision.HIGHEST)
        squares_time_part = jnp.sum(bg_time * bg_time, axis=1)
        pieces = pieces_of(extended_res, block_row)
        project = jnp.einsum(
            "gnt,gktv->gnkv", trace_low, pieces, preferred_element_type=jnp.float32
        )
        correlation = jnp.einsum(
            "gnt,gmt->gnm", traces_now, traces_now, precision=lax.Precision.HIGHEST
        )
        project, correlation, frame_sum, squares_time = lax.psum(
            (project, correlation, frame_part, squares_time_part), "tm"
        )
        inverse = group_inverse(correlation + ridge_foot * all_frames * eye_small)
        moved = jnp.einsum("gnm,gmkv->gnkv", inverse, project, precision=lax.Precision.HIGHEST)
        renewed = jnp.maximum(footprint.astype(jnp.float32) + moved, 0.0).astype(jnp.bfloat16)
        new_space = jnp.maximum(bg_space + frame_sum / (2.0 * squares_time[:, None, None]), 0.0)
        bg_time = jnp.maximum(bg_time + voxel_sum / (2.0 * squares_space[:, None]), 0.0)
        bg_space = new_space
        footprint = renewed
    return (traces_now[None], footprint[None], bg_space, bg_time)


def solution(mesh):
    placed = (
        P("space", "tm", None),
        P("space", None, None, None, None),
        P("space", None, None, "tm"),
        P(None, "space", None),
        P(None, "tm"),
        P("space", None, None),
        P("space", None),
    )
    return jax.shard_map(
        body,
        mesh=mesh,
        in_specs=placed,
        out_specs=(
            P("space", None, None, "tm"),
            P("space", None, None, None, None),
            P(None, "space", None),
            P(None, "tm"),
        ),
        check_vma=False,
    )
```

profile of v0, /device:TPU:6, one launch (start us, length us, event | category | flops | bytes accessed | tf_op | source)
XLA Modules:
  0.0 640.7 jit_solution(14824741590135706060)
XLA Ops:
  10.8 2.1 fusion.141
  13.0 2.1 copy-done.4
  16.0 2.4 collective-permute-start
  33.1 2.6 multiply_reduce_fusion.1
  36.5 11.7 %custom-call.16 = f32[8,16,16]{2,1,0:T(8,128)S(1)} custom-call(f32[8,16,16]{2,1,0:T(8,128)S(1)} %fusion.117), custom_call_target="Cholesky" | custom-call | tf_op jit(solution)/shard_map/jit(cholesky)/cholesky | solution.py:32
  48.5 9.8 %custom-call.17 = f32[8,1,16,16]{2,3,1,0:T(8,128)S(1)} custom-call(f32[8,1,16,16]{3,2,1,0:T(8,128)S(1)} %select_bitcast_fusion.3), custom_call_target="InvertDiagBlocksLowerTriangular" | custom-call | tf_op jit(solution)/shard_map/triangular_solve/custom-call.0 | solution.py:34
  67.1 2.6 slice.706
  69.8 2.4 copy.153
  73.5 5.5 fusion.1
  79.7 6.0 collective-permute-start.2
  88.2 2.6 collective-permute-done.3
  90.9 3.4 pad_maximum_fusion
  94.3 3.3 gather_fusion.2
  109.7 2.1 fusion.140
  112.2 6.3 collective-permute-start.4
  121.8 2.4 copy.158
  129.9 81.3 %all-reduce.1 = (f32[2,32]{1,0:T(2,128)S(1)}, f32[2]{0:T(128)S(1)}) all-reduce(f32[2,32]{1,0:T(2,128)S(1)} %convolution_bitcast_fusion.7, f32[2]{0:T(128)S(1)} %multiply_reduce_fusion.3), channel_id=1, replica_groups=mesh['space'=32,'tm'=8] {'space'}, use_global_device_ids=true, to_apply=%region_14.0 | all-reduce | flops 66 | bytes 528 | tf_op jit(solution)/shard_map/psum | solution.py:117
  215.2 31.1 %all-reduce.3 = (f32[8,16,16]{1,2,0:T(8,128)S(1)}, f32[2]{0:T(128)}) all-reduce(f32[8,16,16]{1,2,0:T(8,128)S(1)} %fusion.222, f32[2]{0:T(128)} %get-tuple-element.370), channel_id=1, replica_groups=mesh['space'=32,'tm'=8] {'tm'}, use_global_device_ids=true, to_apply=%region_11.0 | all-reduce | flops 2050 | bytes 16400 | tf_op jit(solution)/shard_map/psum | solution.py:127
  246.3 3.3 pad_maximum_fusion.1
  249.6 3.4 gather_fusion.3
  256.1 11.7 %custom-call.18 = f32[8,16,16]{2,1,0:T(8,128)S(1)} custom-call(f32[8,16,16]{2,1,0:T(8,128)S(1)} %fusion.112), custom_call_target="Cholesky" | custom-call | tf_op jit(solution)/shard_map/jit(cholesky)/cholesky | solution.py:32
  268.1 9.8 %custom-call.19 = f32[8,1,16,16]{2,3,1,0:T(8,128)S(1)} custom-call(f32[8,1,16,16]{3,2,1,0:T(8,128)S(1)} %select_bitcast_fusion.2), custom_call_target="InvertDiagBlocksLowerTriangular" | custom-call | tf_op jit(solution)/shard_map/triangular_solve/custom-call.0 | solution.py:34
  279.8 56.3 %all-reduce.11.cloned.1.call-done = (f32[8,16,4,512]{3,1,2,0:T(8,128)}, f32[2,64,512]{2,0,1:T(2,128)}) async-done(((f32[8,16,4,512]{3,1,2,0:T(8,128)}, f32[2,64,512]{2,0,1:T(2,128)}), (f32[8,16,4,512]{3,1,2,0:T(8,128)}, f32[2,64,512]{2,0,1:T(2,128)})) %all-reduce.11.cloned.1.call-update) | async-done | bytes 1310736 | tf_op jit(solution)/shard_map/psum | solution.py:127
  336.2 2.3 fusion.10
  338.5 3.5 multiply_reduce_fusion
  351.2 13.0 %custom-call.20 = f32[8,16,16]{2,1,0:T(8,128)} custom-call(f32[8,16,16]{2,1,0:T(8,128)} %fusion.109), custom_call_target="Cholesky" | custom-call | tf_op jit(solution)/shard_map/jit(cholesky)/cholesky | solution.py:32
  366.8 11.2 %custom-call.21 = f32[8,1,16,16]{2,3,1,0:T(8,128)} custom-call(f32[8,1,16,16]{3,2,1,0:T(8,128)} %select_bitcast_fusion.1), custom_call_target="InvertDiagBlocksLowerTriangular" | custom-call | tf_op jit(solution)/shard_map/triangular_solve/custom-call.0 | solution.py:34
  378.0 2.8 copy.162
  380.8 2.1 fusion.139
  390.5 2.3 slice.720
  410.0 4.6 copy.163
  416.6 5.6 fusion.5
  422.2 5.1 collective-permute-start.10
  429.0 3.8 collective-permute-done.11
  434.5 3.4 gather_fusion.4
  449.6 31.8 %all-reduce.2 = (f32[8,16,16]{1,2,0:T(8,128)S(1)}, f32[2]{0:T(128)}) all-reduce(f32[8,16,16]{1,2,0:T(8,128)S(1)} %fusion.224, f32[2]{0:T(128)S(1)} %copy-done.58), channel_id=1, replica_groups=mesh['space'=32,'tm'=8] {'tm'}, use_global_device_ids=true, to_apply=%region_20.0 | all-reduce | flops 2050 | bytes 16400 | tf_op jit(solution)/shard_map/psum | solution.py:127
  482.1 2.8 copy.167
  484.9 2.1 fusion.138
  487.1 2.1 copy-done.5
  492.8 12.4 %custom-call.22 = f32[8,16,16]{2,1,0:T(8,128)S(1)} custom-call(f32[8,16,16]{2,1,0:T(8,128)} %fusion.106), custom_call_target="Cholesky" | custom-call | tf_op jit(solution)/shard_map/jit(cholesky)/cholesky | solution.py:32
  507.4 2.6 slice.727
  510.0 2.4 copy.168
  515.0 10.2 %collective-permute-start.14 = (bf16[4,32,512]{2,1,0:T(8,128)(2,1)S(1)}, bf16[4,32,512]{2,1,0:T(8,128)(2,1)S(1)}, u32[]{:S(2)}, u32[]{:S(2)}) collective-permute-start(bf16[4,32,512]{2,1,0:T(8,128)(2,1)S(1)} %get-tuple-element.347), channel_id=1, source_target_pairs={{0,8},{8,16},{16,24},{24,32},{32,40},{40,48},{48,56},{56,64},{64,7... | collective-permute-start | bytes 393224 | tf_op jit(solution)/shard_map/ppermute | solution.py:23
  530.3 2.4 gather_fusion.5
  534.2 9.8 %custom-call.23 = f32[8,1,16,16]{2,3,1,0:T(8,128)S(1)} custom-call(f32[8,1,16,16]{3,2,1,0:T(8,128)S(1)} %select_bitcast_fusion), custom_call_target="InvertDiagBlocksLowerTriangular" | custom-call | tf_op jit(solution)/shard_map/triangular_solve/custom-call.0 | solution.py:34
  546.5 79.9 %all-reduce = (f32[2,32]{1,0:T(2,128)S(1)}, f32[2]{0:T(128)S(1)}) all-reduce(f32[2,32]{1,0:T(2,128)S(1)} %convolution_bitcast_fusion.6, f32[2]{0:T(128)S(1)} %copy-done.60), channel_id=1, replica_groups=mesh['space'=32,'tm'=8] {'space'}, use_global_device_ids=true, to_apply=%region_25.0 | all-reduce | flops 66 | bytes 528 | tf_op jit(solution)/shard_map/psum | solution.py:117
  627.0 2.1 all-reduce.9.cloned.1.call-done
  629.1 2.3 fusion.12
  (364 shorter events, 122.0 us)
Async XLA Ops:
  7.2 329.0 %all-reduce.11.cloned.1.call-start = ((), (), s32[]{:S(2)}) async-start(), calls=%async_computation.1 | async-start | bytes 2621440 | tf_op jit(solution)/shard_map/psum | solution.py:127
  8.0 13.7 %copy-start.46 = (s32[32]{0:T(128)}, s32[32]{0:T(128)S(1)}, u32[]{:S(2)}) copy-start(s32[32]{0:T(128)S(1)} %eq.76) | copy-start | bytes 388
  15.1 17.7 %copy-start.57 = (s32[1,8,4]{1,2,0:T(4,128)S(1)}, s32[1,8,4]{1,2,0:T(4,128)}, u32[]{:S(2)}) copy-start(s32[1,8,4]{1,2,0:T(4,128)} %param.65) | copy-start | bytes 388
  15.1 17.9 %copy-start.11 = (bf16[1,8,16,4,512]{4,3,2,1,0:T(4,128)(2,1)S(1)}, bf16[1,8,16,4,512]{4,3,2,1,0:T(4,128)(2,1)}, u32[]{:S(2)}) copy-start(bf16[1,8,16,4,512]{4,3,2,1,0:T(4,128)(2,1)} %param.61) | copy-start | bytes 1572868
  16.0 56.2 %collective-permute-start = (f32[4,32,512]{2,1,0:T(8,128)}, f32[4,32,512]{2,1,0:T(8,128)}, u32[]{:S(2)}, u32[]{:S(2)}) collective-permute-start(f32[4,32,512]{2,1,0:T(8,128)} %bitcast.629), channel_id=1, source_target_pairs={{0,8},{8,16},{16,24},{24,32},{32,40},{40,48},{48,56},{56,64},{64,7... | collective-permute-start | bytes 786440 | tf_op jit(solution)/shard_map/ppermute | solution.py:23
  19.3 54.0 %collective-permute-start.1 = (f32[4,32,512]{2,1,0:T(8,128)}, f32[4,32,512]{2,1,0:T(8,128)S(1)}, u32[]{:S(2)}, u32[]{:S(2)}) collective-permute-start(f32[4,32,512]{2,1,0:T(8,128)} %bitcast.628), channel_id=1, source_target_pairs={{8,0},{16,8},{24,16},{32,24},{40,32},{48,40},{56,48},{64,56},{72,6... | collective-permute-start | bytes 786440 | tf_op jit(solution)/shard_map/ppermute | solution.py:26
  21.2 14.6 %copy-start.27 = (s32[8]{0:T(128)}, s32[8]{0:T(128)S(1)}, u32[]{:S(2)}) copy-start(s32[8]{0:T(128)S(1)} %or_bitcast_fusion) | copy-start | bytes 100
  21.2 27.1 %copy-start.33 = (pred[16,16]{1,0:T(8,128)(4,1)}, pred[16,16]{1,0:T(8,128)(4,1)S(1)}, u32[]{:S(2)}) copy-start(pred[16,16]{1,0:T(8,128)(4,1)S(1)} %iota_compare_fusion.6) | copy-start | bytes 772
  21.2 27.2 %copy-start.30 = (pred[16,16]{1,0:T(8,128)(4,1)}, pred[16,16]{1,0:T(8,128)(4,1)S(1)}, u32[]{:S(2)}) copy-start(pred[16,16]{1,0:T(8,128)(4,1)S(1)} %iota_compare_fusion.5) | copy-start | bytes 772
  33.1 31.7 %copy-start.59 = (s32[3]{0:T(128)S(1)}, s32[3]{0:T(128)}, u32[]{:S(2)}) copy-start(s32[3]{0:T(128)} %constant.554.clone.1) | copy-start | bytes 40
  35.7 34.1 %copy-start.15 = (f32[8,16,8,16]{3,1,2,0:T(8,128)}, f32[8,16,8,16]{3,1,2,0:T(8,128)S(1)}, u32[]{:S(2)}) copy-start(f32[8,16,8,16]{3,1,2,0:T(8,128)S(1)} %multiply_reduce_fusion.1) | copy-start | bytes 196612
  73.4 13.9 %copy-start.10 = (f32[1,8,16,32]{3,2,1,0:T(8,128)S(1)}, f32[1,8,16,32]{3,2,1,0:T(8,128)}, u32[]{:S(2)}) copy-start(f32[1,8,16,32]{3,2,1,0:T(8,128)} %param.62) | copy-start | bytes 49156
  73.4 14.0 %copy-start.25 = (f32[1,16,8,16]{3,1,2,0:T(8,128)S(1)}, f32[1,16,8,16]{3,1,2,0:T(8,128)}, u32[]{:S(2)}) copy-start(f32[1,16,8,16]{3,1,2,0:T(8,128)} %get-tuple-element.364) | copy-start | bytes 24580
  73.4 14.1 %copy-start.24 = (f32[1,16,8,16]{3,1,2,0:T(8,128)S(1)}, f32[1,16,8,16]{3,1,2,0:T(8,128)}, u32[]{:S(2)}) copy-start(f32[1,16,8,16]{3,1,2,0:T(8,128)} %get-tuple-element.365) | copy-start | bytes 24580
  73.4 14.2 %copy-start.23 = (f32[1,16,8,16]{3,1,2,0:T(8,128)S(1)}, f32[1,16,8,16]{3,1,2,0:T(8,128)}, u32[]{:S(2)}) copy-start(f32[1,16,8,16]{3,1,2,0:T(8,128)} %get-tuple-element.366) | copy-start | bytes 24580
  73.4 14.3 %copy-start.22 = (f32[1,16,8,16]{3,1,2,0:T(8,128)S(1)}, f32[1,16,8,16]{3,1,2,0:T(8,128)}, u32[]{:S(2)}) copy-start(f32[1,16,8,16]{3,1,2,0:T(8,128)} %get-tuple-element.367) | copy-start | bytes 24580
  73.4 14.4 %copy-start.21 = (f32[1,16,8,16]{3,1,2,0:T(8,128)S(1)}, f32[1,16,8,16]{3,1,2,0:T(8,128)}, u32[]{:S(2)}) copy-start(f32[1,16,8,16]{3,1,2,0:T(8,128)} %get-tuple-element.368) | copy-start | bytes 24580
  79.0 8.3 %copy-start.9 = (bf16[64,32,512]{2,1,0:T(8,128)(2,1)}, bf16[64,32,512]{2,1,0:T(8,128)(2,1)S(1)}, u32[]{:S(2)}) copy-start(bf16[64,32,512]{2,1,0:T(8,128)(2,1)S(1)} %get-tuple-element.383) | copy-start | bytes 6291460
  79.7 8.5 %collective-permute-start.2 = (bf16[4,32,512]{2,1,0:T(8,128)(2,1)}, bf16[4,32,512]{2,1,0:T(8,128)(2,1)}, u32[]{:S(2)}, u32[]{:S(2)}) collective-permute-start(bf16[4,32,512]{2,1,0:T(8,128)(2,1)} %get-tuple-element.353), channel_id=1, source_target_pairs={{0,8},{8,16},{16,24},{24,32},{32,40},{40,48},{48,56},{56,64},{64,7... | collective-permute-start | bytes 393224 | tf_op jit(solution)/shard_map/ppermute | solution.py:23
  85.8 5.1 collective-permute-start.3
  88.2 9.3 %copy-start.53 = (pred[32]{0:T(512)(128)(4,1)S(1)}, pred[32]{0:T(512)(128)(4,1)}, u32[]{:S(2)}) copy-start(pred[32]{0:T(512)(128)(4,1)} %compare_and_fusion) | copy-start | bytes 100
  112.2 12.0 %collective-permute-start.4 = (f32[4,32,512]{2,1,0:T(8,128)S(1)}, f32[4,32,512]{2,1,0:T(8,128)S(1)}, u32[]{:S(2)}, u32[]{:S(2)}) collective-permute-start(f32[4,32,512]{2,1,0:T(8,128)S(1)} %bitcast.681), channel_id=1, source_target_pairs={{0,8},{8,16},{16,24},{24,32},{32,40},{40,48},{48,56},{56,64},{64,7... | collective-permute-start | bytes 786440 | tf_op jit(solution)/shard_map/ppermute | solution.py:23
  118.5 5.8 collective-permute-start.5
  211.2 35.0 %collective-permute-start.6 = (bf16[4,32,512]{2,1,0:T(8,128)(2,1)}, bf16[4,32,512]{2,1,0:T(8,128)(2,1)S(1)}, u32[]{:S(2)}, u32[]{:S(2)}) collective-permute-start(bf16[4,32,512]{2,1,0:T(8,128)(2,1)} %get-tuple-element.351), channel_id=1, source_target_pairs={{0,8},{8,16},{16,24},{24,32},{32,40},{40,48},{48,56},{56,64},{64,7... | collective-permute-start | bytes 393224 | tf_op jit(solution)/shard_map/ppermute | solution.py:23
  212.5 33.8 %collective-permute-start.7 = (bf16[4,32,512]{2,1,0:T(8,128)(2,1)S(1)}, bf16[4,32,512]{2,1,0:T(8,128)(2,1)S(1)}, u32[]{:S(2)}, u32[]{:S(2)}) collective-permute-start(bf16[4,32,512]{2,1,0:T(8,128)(2,1)S(1)} %get-tuple-element.352), channel_id=1, source_target_pairs={{8,0},{16,8},{24,16},{32,24},{40,32},{48,40},{56,48},{64,56},{72,6... | collective-permute-start | bytes 393224 | tf_op jit(solution)/shard_map/ppermute | solution.py:26
  254.4 13.4 %copy-start.34 = (pred[16,16]{1,0:T(8,128)(4,1)S(1)}, pred[16,16]{1,0:T(8,128)(4,1)}, u32[]{:S(2)}) copy-start(pred[16,16]{1,0:T(8,128)(4,1)} %copy-done.33) | copy-start | bytes 772
  254.4 13.6 %copy-start.31 = (pred[16,16]{1,0:T(8,128)(4,1)S(1)}, pred[16,16]{1,0:T(8,128)(4,1)}, u32[]{:S(2)}) copy-start(pred[16,16]{1,0:T(8,128)(4,1)} %copy-done.30) | copy-start | bytes 772
  254.4 24.8 %copy-start.63 = (f32[2]{0:T(128)S(1)}, f32[2]{0:T(128)}, u32[]{:S(2)}) copy-start(f32[2]{0:T(128)} %get-tuple-element.326) | copy-start | bytes 28
  255.7 373.5 %all-reduce.9.cloned.1.call-start = ((), (), s32[]{:S(2)}) async-start(), calls=%async_computation | async-start | bytes 2621440 | tf_op jit(solution)/shard_map/psum | solution.py:127
  342.0 38.8 %copy-start.13 = (f32[8,16,8,16]{3,1,2,0:T(8,128)}, f32[8,16,8,16]{3,1,2,0:T(8,128)S(1)}, u32[]{:S(2)}) copy-start(f32[8,16,8,16]{3,1,2,0:T(8,128)S(1)} %multiply_reduce_fusion) | copy-start | bytes 196612
  384.7 29.8 %collective-permute-start.8 = (f32[4,32,512]{2,1,0:T(8,128)}, f32[4,32,512]{2,1,0:T(8,128)}, u32[]{:S(2)}, u32[]{:S(2)}) collective-permute-start(f32[4,32,512]{2,1,0:T(8,128)} %bitcast.625), channel_id=1, source_target_pairs={{0,8},{8,16},{16,24},{24,32},{32,40},{40,48},{48,56},{56,64},{64,7... | collective-permute-start | bytes 786440 | tf_op jit(solution)/shard_map/ppermute | solution.py:23
  386.7 28.9 %collective-permute-start.9 = (f32[4,32,512]{2,1,0:T(8,128)}, f32[4,32,512]{2,1,0:T(8,128)}, u32[]{:S(2)}, u32[]{:S(2)}) collective-permute-start(f32[4,32,512]{2,1,0:T(8,128)} %bitcast.624), channel_id=1, source_target_pairs={{8,0},{16,8},{24,16},{32,24},{40,32},{48,40},{56,48},{64,56},{72,6... | collective-permute-start | bytes 786440 | tf_op jit(solution)/shard_map/ppermute | solution.py:26
  422.2 6.7 %collective-permute-start.10 = (bf16[4,32,512]{2,1,0:T(8,128)(2,1)S(1)}, bf16[4,32,512]{2,1,0:T(8,128)(2,1)S(1)}, u32[]{:S(2)}, u32[]{:S(2)}) collective-permute-start(bf16[4,32,512]{2,1,0:T(8,128)(2,1)S(1)} %get-tuple-element.349), channel_id=1, source_target_pairs={{0,8},{8,16},{16,24},{24,32},{32,40},{40,48},{48,56},{56,64},{64,7... | collective-permute-start | bytes 393224 | tf_op jit(solution)/shard_map/ppermute | solution.py:23
  427.3 5.4 collective-permute-start.11
  428.9 8.9 %copy-start.55 = (pred[32]{0:T(512)(128)(4,1)S(1)}, pred[32]{0:T(512)(128)(4,1)}, u32[]{:S(2)}) copy-start(pred[32]{0:T(512)(128)(4,1)} %compare_and_fusion) | copy-start | bytes 100
  441.7 7.8 %copy-start.58 = (f32[2]{0:T(128)S(1)}, f32[2]{0:T(128)}, u32[]{:S(2)}) copy-start(f32[2]{0:T(128)} %get-tuple-element.333) | copy-start | bytes 28
  447.5 85.4 %copy-start.8 = (f32[8,16,32]{2,1,0:T(8,128)}, f32[8,16,32]{2,1,0:T(8,128)S(1)}, u32[]{:S(2)}) copy-start(f32[8,16,32]{2,1,0:T(8,128)S(1)} %fusion.77) | copy-start | bytes 49156
  449.6 35.3 %copy-start.49 = (s32[32]{0:T(128)S(1)}, s32[32]{0:T(128)}, u32[]{:S(2)}) copy-start(s32[32]{0:T(128)} %copy-done.46) | copy-start | bytes 388
  484.9 7.2 %copy-start.18 = (f32[8,16,16]{2,1,0:T(8,128)S(1)}, f32[8,16,16]{2,1,0:T(8,128)}, u32[]{:S(2)}) copy-start(f32[8,16,16]{2,1,0:T(8,128)} %copy.126) | copy-start | bytes 24580
  490.1 22.3 %collective-permute-start.12 = (f32[4,32,512]{2,1,0:T(8,128)}, f32[4,32,512]{2,1,0:T(8,128)}, u32[]{:S(2)}, u32[]{:S(2)}) collective-permute-start(f32[4,32,512]{2,1,0:T(8,128)} %bitcast.623), channel_id=1, source_target_pairs={{0,8},{8,16},{16,24},{24,32},{32,40},{40,48},{48,56},{56,64},{64,7... | collective-permute-start | bytes 786440 | tf_op jit(solution)/shard_map/ppermute | solution.py:23
  505.3 8.2 %collective-permute-start.13 = (f32[4,32,512]{2,1,0:T(8,128)S(1)}, f32[4,32,512]{2,1,0:T(8,128)S(1)}, u32[]{:S(2)}, u32[]{:S(2)}) collective-permute-start(f32[4,32,512]{2,1,0:T(8,128)S(1)} %bitcast.680), channel_id=1, source_target_pairs={{8,0},{16,8},{24,16},{32,24},{40,32},{48,40},{56,48},{64,56},{72,6... | collective-permute-start | bytes 786440 | tf_op jit(solution)/shard_map/ppermute | solution.py:26
  513.6 13.2 %copy-start.45 = (f32[2,32]{1,0:T(2,128)S(1)}, f32[2,32]{1,0:T(2,128)}, u32[]{:S(2)}) copy-start(f32[2,32]{1,0:T(2,128)} %get-tuple-element.334) | copy-start | bytes 772
  515.0 13.5 %copy-start.1 = (bf16[64,32,512]{2,1,0:T(8,128)(2,1)}, bf16[64,32,512]{2,1,0:T(8,128)(2,1)S(1)}, u32[]{:S(2)}) copy-start(bf16[64,32,512]{2,1,0:T(8,128)(2,1)S(1)} %fusion.7) | copy-start | bytes 6291460
  515.0 13.4 %collective-permute-start.14 = (bf16[4,32,512]{2,1,0:T(8,128)(2,1)S(1)}, bf16[4,32,512]{2,1,0:T(8,128)(2,1)S(1)}, u32[]{:S(2)}, u32[]{:S(2)}) collective-permute-start(bf16[4,32,512]{2,1,0:T(8,128)(2,1)S(1)} %get-tuple-element.347), channel_id=1, source_target_pairs={{0,8},{8,16},{16,24},{24,32},{32,40},{40,48},{48,56},{56,64},{64,7... | collective-permute-start | bytes 393224 | tf_op jit(solution)/shard_map/ppermute | solution.py:23
  525.3 3.2 collective-permute-start.15
  532.8 11.9 %copy-start.62 = (f32[2]{0:T(128)S(1)}, f32[2]{0:T(128)}, u32[]{:S(2)}) copy-start(f32[2]{0:T(128)} %get-tuple-element.324) | copy-start | bytes 28
  532.9 11.9 %copy-start.2 = (bf16[64,32,512]{2,1,0:T(8,128)(2,1)S(1)}, bf16[64,32,512]{2,1,0:T(8,128)(2,1)}, u32[]{:S(2)}) copy-start(bf16[64,32,512]{2,1,0:T(8,128)(2,1)} %copy-done.1) | copy-start | bytes 6291460
  534.1 12.4 %copy-start.60 = (f32[2]{0:T(128)S(1)}, f32[2]{0:T(128)}, u32[]{:S(2)}) copy-start(f32[2]{0:T(128)} %get-tuple-element.331) | copy-start | bytes 28
  (34 other events, 141.8 us)
Sparse Core Ops, SparseCore 0:
  255.8 80.3 all-reduce.10
  534.3 94.8 all-reduce.8
where the time goes:
time: 649 us; the launch traced here: 641 us
  blocking collectives  224 us (35%)
  other arithmetic  126 us (19%)
  local copies, waits for them, and re-layouts  80.4 us (12%)
  matrix products  66 us (10%)
  waiting for transfers between devices  65 us (10%)
  starting transfers between devices  47.7 us (7%)
  between operations  31.4 us (5%)
    psum x2, blocking collectives, body(): lax.psum((voxel_part, squares_space_part), 'space')  161 us
    psum x2, blocking collectives, body(): lax.psum((project, correlation, frame_part, squares_time_part), 'tm')  62.9 us
    psum x2, waiting for transfers between devices, body(): lax.psum((project, correlation, frame_part, squares_time_part), 'tm')  58.4 us
    another operation x13, other arithmetic, group_inverse(): lower_factor = jnp.linalg.cholesky(matrices)  51 us
    another operation x9, other arithmetic, group_inverse(): lax.linalg.triangular_solve(lower_factor, identity, left_side=True, lower...  42.6 us
    ppermute x8, starting transfers between devices, with_halo(): lax.ppermute(lax.slice_in_dim(block, block.shape[dim] - width, None, axis...  35.4 us
    unnamed x149, local copies, waits for them, and re-layouts  31.3 us
  transfers between devices with their start and end apart: 18, of which 5 were waited for; matrix products, arithmetic and copies ran while one was open for 20% of the time, Pallas kernels for 0%

commit v1 on v0

v1 whole, which is shorter than its diff:
```python
import functools

import jax
import jax.numpy as jnp
from jax import lax
from jax.experimental import pallas as pl
from jax.experimental.pallas import tpu as pltpu
from jax.sharding import PartitionSpec as P

MESH = pl.DeviceIdType.MESH
HIGH = lax.Precision.HIGHEST
F32 = jnp.float32
BF16 = jnp.bfloat16

G = 16
NG = 8
NC = NG * G
BPG = 4
BV = 512
VB = 64
EXT = 72
FR = 32
NT = 8
ROUNDS = 2
RIDGE_TRACE = 0.01 * BPG * BV
RIDGE_FOOT = 0.1 * FR * NT


def dot(a, b, precision=None):
    return lax.dot_general(a, b, (((1,), (0,)), ((), ())), precision=precision, preferred_element_type=F32)


def dot_nt(a, b, precision=None):
    return lax.dot_general(a, b, (((1,), (1,)), ((), ())), precision=precision, preferred_element_type=F32)


def split3(x):
    hi = x.astype(BF16).astype(F32)
    rest = x - hi
    mid = rest.astype(BF16).astype(F32)
    return hi, mid, rest - mid


def lanes(rows):
    return lax.broadcasted_iota(jnp.int32, (rows, NC), 1)


def fold_diagonal(square):
    group = lanes(G) // G
    out = jnp.zeros((G, NC), F32)
    for h in range(NG):
        out = out + jnp.where(group == h, square[h * G : (h + 1) * G], 0.0)
    return out


def spread_diagonal(folded):
    group = lanes(G) // G
    return jnp.concatenate([jnp.where(group == h, folded, 0.0) for h in range(NG)], axis=0)


def inverse_blocks(folded, ridge):
    first = lanes(G) % G
    sub = lax.broadcasted_iota(jnp.int32, (G, NC), 0)
    folded = folded + jnp.where(sub == first, ridge, 0.0)
    rows = []
    for n in range(G):
        moved = folded if n == 0 else pltpu.roll(folded, NC - n, 1)
        rows.append(jnp.where(first == 0, moved, jnp.where(sub == n, 1.0, 0.0)))
    for p in range(G):
        pivot = 1.0 / rows[p][p : p + 1]
        at = sub == p
        scaled = jnp.where(at, jnp.broadcast_to(pivot, (G, NC)), rows[p] * pivot)
        for n in range(G):
            if n != p:
                rows[n] = jnp.where(at, 0.0, rows[n]) - rows[n][p : p + 1] * scaled
        rows[p] = scaled
    out = jnp.zeros((G, NC), F32)
    for n in range(G):
        moved = rows[n] if n == 0 else pltpu.roll(rows[n], n, 1)
        out = jnp.where(first == n, moved, out)
    return spread_diagonal(out)


def kernel(
    nsp, levels,
    act, f0, tr0, bg0, bt0, bl, order,
    out_tr, out_f, out_bg, out_bt,
    blrow, res, pieces, foot, bgs, bts, halo_f, halo_out, tl_in, tl_out, corr_out, corr_in, sb, rb, vacc, vox, bgn, zs, btm,
    nb_s, nb_r, tm_s, tm_r, vx_s, vx_r,
):
    me = lax.axis_index("tm")
    sp = lax.axis_index("space")
    left = lax.rem(sp + nsp - 1, nsp)
    right = lax.rem(sp + 1, nsp)
    peers = []
    for stride, size in levels:
        q = lax.rem(sp // stride, size)
        row = []
        for d in range(1, size):
            other = lax.rem(q + d, size)
            row.append((sp + (other - q) * stride, other))
        peers.append((q, row))

    barrier = pltpu.get_barrier_semaphore()
    count = 0
    for d in range(1, NT):
        pl.semaphore_signal(barrier, inc=1, device_id=(sp, lax.rem(me + d, NT)), device_id_type=MESH)
        count += 1
    for other in (left, right):
        pl.semaphore_signal(barrier, inc=1, device_id=(other, me), device_id_type=MESH)
        count += 1
    for _, row in peers:
        for other, _ in row:
            pl.semaphore_signal(barrier, inc=1, device_id=(other, me), device_id_type=MESH)
            count += 1

    sends = []

    def send(src, dst, ssem, rsem, device):
        copy = pltpu.make_async_remote_copy(
            src_ref=src, dst_ref=dst, send_sem=ssem, recv_sem=rsem, device_id=device, device_id_type=MESH
        )
        copy.start()
        sends.append(copy)

    def arrived(ref, ssem, rsem, device):
        pltpu.make_async_remote_copy(
            src_ref=ref, dst_ref=ref, send_sem=ssem, recv_sem=rsem, device_id=device, device_id_type=MESH
        ).wait_recv()

    def to_neighbours(cat, src_left, src_right, dst):
        send(src_right, dst(0), nb_s.at[cat, 0], nb_r.at[cat, 0], (right, me))
        send(src_left, dst(1), nb_s.at[cat, 1], nb_r.at[cat, 1], (left, me))

    def from_neighbours(cat, dst):
        arrived(dst(0), nb_s.at[cat, 0], nb_r.at[cat, 0], (left, me))
        arrived(dst(1), nb_s.at[cat, 1], nb_r.at[cat, 1], (right, me))

    entry = [[bl[g, k] for k in range(BPG)] for g in range(NG)]
    group32 = lanes(FR) // G

    for k in range(BPG):
        row = jnp.zeros((FR, NC), jnp.int32)
        for g in range(NG):
            row = jnp.where(group32 == g, entry[g][k], row)
        blrow[:, k * NC : (k + 1) * NC] = row
    halo_id = jnp.full((G, NC), -1, jnp.int32)
    halo_k = []
    group16 = lanes(G) // G
    for g in range(NG):
        hid = jnp.int32(-1)
        hk = jnp.int32(0)
        for k in range(BPG):
            out = jnp.logical_or(entry[g][k] < 4, entry[g][k] >= 68)
            hid = jnp.where(out, entry[g][k], hid)
            hk = jnp.where(out, k, hk)
        halo_id = jnp.where(group16 == g, hid, halo_id)
        halo_k.append(hk)
    halo_bf = halo_id.astype(F32).astype(BF16)

    def stage_halo(r, source):
        for g in range(NG):
            halo_out[r, g * G : (g + 1) * G, :] = source[halo_k[g], g * G : (g + 1) * G, :]

    def stage_traces(i, low):
        tl_out[i, 0:FR, :] = low
        tl_out[i, FR : FR + G, :] = halo_bf

    def gram_of(source):
        everything = source[...].reshape(BPG * NC, BV)
        total = jnp.zeros((NC, NC), F32)
        for k in range(BPG):
            product = dot_nt(source[k], everything)
            column = jnp.concatenate([jnp.full((G, NC), entry[g][k], jnp.int32) for g in range(NG)], axis=0)
            for j in range(BPG):
                row = blrow[:, j * NC : (j + 1) * NC]
                row = jnp.concatenate([row] * (NC // FR), axis=0)
                total = total + jnp.where(column == row, product[:, j * NC : (j + 1) * NC], 0.0)
        return total

    def chunk(inst, j, source, space, low4, traces_i, r, side, with_bg):
        parts = []
        for i in range(8):
            parts.append(jnp.where(blrow[...] == 8 * j + 4 + i, low4, 0.0).astype(BF16))
        lhs = jnp.concatenate(parts, axis=0)
        rebuilt = dot(lhs, source[...].reshape(BPG * NC, BV))
        if side is not None:
            low = tl_in[traces_i, side, 0:FR, :].astype(F32)
            hid = tl_in[traces_i, side, FR : FR + G, :].astype(F32)
            hid = jnp.concatenate([hid, hid], axis=0)
            base = 68.0 if side == 0 else 0.0
            near = jnp.concatenate(
                [jnp.where(hid == base + i, low, 0.0).astype(BF16) for i in range(4)], axis=0
            )
            near = dot(near, halo_f[r, side])
            if side == 0:
                rebuilt = jnp.concatenate([rebuilt[: 4 * FR] + near, rebuilt[4 * FR :]], axis=0)
            else:
                rebuilt = jnp.concatenate([rebuilt[: 4 * FR], rebuilt[4 * FR :] + near], axis=0)
        t0 = jnp.concatenate([bts[0]] * (BV // NC), axis=1)
        t1 = jnp.concatenate([bts[1]] * (BV // NC), axis=1)
        s0 = space[0, pl.ds(8 * j, 8), :]
        s1 = space[1, pl.ds(8 * j, 8), :]
        out = []
        for i in range(8):
            backdrop = s0[i : i + 1] * t0 + s1[i : i + 1] * t1
            seen = act[8 * j + i].astype(F32)
            value = ((seen - rebuilt[i * FR : (i + 1) * FR]) - backdrop).astype(BF16)
            res[inst, 8 * j + 4 + i] = value
            out.append(value)
        if with_bg:
            flat = jnp.concatenate(out, axis=0)
            frame = dot(btm[...], flat)
            sb[r, j, 64:80, :] = (frame[0:16] + frame[16:32] + frame[32:48]).astype(BF16)
            s = jnp.concatenate([s0, s1], axis=0)
            s = jnp.concatenate([x.astype(BF16) for x in split3(s)], axis=0)
            vacc[...] += dot_nt(flat, s)

    def residual(inst, source, space, low, traces_i, r, with_bg):
        low4 = jnp.concatenate([low.astype(F32)] * BPG, axis=1)
        chunk(inst, 0, source, space, low4, traces_i, r, 0, with_bg)
        chunk(inst, 7, source, space, low4, traces_i, r, 1, with_bg)
        cat = 5 + inst
        send(res.at[inst, pl.ds(64, 4)], res.at[inst, pl.ds(0, 4)], nb_s.at[cat, 0], nb_r.at[cat, 0], (right, me))
        send(res.at[inst, pl.ds(4, 4)], res.at[inst, pl.ds(68, 4)], nb_s.at[cat, 1], nb_r.at[cat, 1], (left, me))

        def body(j, carry):
            chunk(inst, j, source, space, low4, traces_i, r, None, with_bg)
            return carry

        lax.fori_loop(1, 7, body, 0)

    def gather(inst):
        cat = 5 + inst
        arrived(res.at[inst, pl.ds(0, 4)], nb_s.at[cat, 0], nb_r.at[cat, 0], (left, me))
        arrived(res.at[inst, pl.ds(68, 4)], nb_s.at[cat, 1], nb_r.at[cat, 1], (right, me))
        for g in range(NG):
            for k in range(BPG):
                pieces[k, g * FR : (g + 1) * FR, :] = res[inst, entry[g][k]]

    traces_now = tr0[...]
    bts[...] = bt0[...]
    low = traces_now.astype(BF16)
    stage_halo(0, f0)
    stage_traces(0, low)

    pl.semaphore_wait(barrier, count)
    to_neighbours(0, halo_out.at[0], halo_out.at[0], lambda s: halo_f.at[0, s])
    to_neighbours(2, tl_out.at[0], tl_out.at[0], lambda s: tl_in.at[0, s])

    for r in range(ROUNDS):
        source = f0 if r == 0 else foot.at[0]
        space = bg0 if r == 0 else bgs.at[0]
        gram = gram_of(source)
        inverse = inverse_blocks(fold_diagonal(gram), RIDGE_TRACE)
        weights = dot(gram, inverse, HIGH)

        from_neighbours(r, lambda s: halo_f.at[r, s])
        if r == 0:
            from_neighbours(2, lambda s: tl_in.at[0, s])
        residual(2 * r, source, space, low, r, r, False)
        gather(2 * r)
        cross = jnp.zeros((NG * FR, NC), F32)
        for k in range(BPG):
            cross = cross + dot_nt(pieces[k], source[k])
        drives = jnp.zeros((FR, NC), F32)
        for g in range(NG):
            drives = drives + jnp.where(group32 == g, cross[g * FR : (g + 1) * FR], 0.0)
        drives = dot(drives, inverse, HIGH)
        current = traces_now
        for p in range(NG):
            fresh = jnp.maximum(current + (drives - dot(current - traces_now, weights, HIGH)), 0.0)
            current = jnp.where(group32 == order[p], fresh, current)
        traces_now = current
        low = traces_now.astype(BF16)

        stage_traces(r + 1, low)
        to_neighbours(3 + r, tl_out.at[r + 1], tl_out.at[r + 1], lambda s: tl_in.at[r + 1, s])
        corr = lax.dot_general(
            traces_now, traces_now, (((0,), (0,)), ((), ())), precision=HIGH, preferred_element_type=F32
        )
        sq = [jnp.sum(bts[c] * bts[c], axis=0, keepdims=True) for c in range(2)]
        corr_out[r, 0:G, :] = fold_diagonal(corr)
        corr_out[r, G : G + 4, :] = jnp.broadcast_to(sq[0], (4, NC))
        corr_out[r, G + 4 : G + 8, :] = jnp.broadcast_to(sq[1], (4, NC))
        for d in range(1, NT):
            to = lax.rem(me + d, NT)
            send(corr_out.at[r], corr_in.at[r, me], tm_s.at[0, r, to], tm_r.at[0, r, me], (sp, to))

        lane = lanes(FR)
        spread = jnp.zeros((FR, NC), F32)
        for c in range(2):
            for s, part in enumerate(split3(bts[c])):
                spread = jnp.where(lane // 8 == s * 2 + c, part, spread)
        stacked = jnp.concatenate(
            [jnp.where(lane % 8 == b, spread, 0.0).astype(BF16) for b in range(8)], axis=0
        )
        eye = (
            lax.broadcasted_iota(jnp.int32, (48, NC), 0) == lax.broadcasted_iota(jnp.int32, (48, NC), 1)
        ).astype(F32).astype(BF16)
        btm[...] = dot_nt(eye, stacked).astype(BF16)
        vacc[...] = jnp.zeros_like(vacc)

        from_neighbours(3 + r, lambda s: tl_in.at[r + 1, s])
        residual(2 * r + 1, source, space, low, r + 1, r, True)

        row = lax.broadcasted_iota(jnp.int32, (FR, 48), 0)
        col = lax.broadcasted_iota(jnp.int32, (FR, 48), 1)
        summed = jnp.zeros((FR, 48), F32)
        for b in range(8):
            summed = summed + jnp.where(col % 8 == b, vacc[b * FR : (b + 1) * FR, :], 0.0)
        packed = jnp.zeros((FR, NC), F32)
        for c in range(2):
            total = jnp.sum(jnp.where((col // 8) % 2 == c, summed, 0.0), axis=1, keepdims=True)
            packed = jnp.where(lane == c, total, packed)
            field = space[c]
            squares = jnp.sum(jnp.sum(field * field, axis=0, keepdims=True), axis=1, keepdims=True)
            packed = jnp.where(lane == 2 + c, squares, packed)

        def level_send(i, value):
            q, rows = peers[i]
            vox[r, i, q] = value
            for other, oq in rows:
                send(vox.at[r, i, q], vox.at[r, i, q], vx_s.at[r, i, oq], vx_r.at[r, i, q], (other, me))

        def level_sum(i):
            q, rows = peers[i]
            for other, oq in rows:
                arrived(vox.at[r, i, oq], vx_s.at[r, i, oq], vx_r.at[r, i, oq], (other, me))
            total = vox[r, i, 0]
            for s in range(1, levels[i][1]):
                total = total + vox[r, i, s]
            return total

        level_send(0, packed)

        for d in range(1, NT):
            other = lax.rem(me + d, NT)
            arrived(corr_in.at[r, other], tm_s.at[0, r, other], tm_r.at[0, r, other], (sp, other))
        corr_in[r, me] = corr_out[r]
        total = corr_in[r, 0]
        for s in range(1, NT):
            total = total + corr_in[r, s]
        inverse_a = inverse_blocks(total[0:G], RIDGE_FOOT)
        square_time = [total[G : G + 1], total[G + 4 : G + 5]]
        masked = jnp.concatenate(
            [jnp.where(group32 == g, low.astype(F32), 0.0) for g in range(NG)], axis=0
        )
        z = dot_nt(inverse_a, masked, HIGH)
        z_high = z.astype(BF16)
        zs[0] = z_high
        zs[1] = (z - z_high.astype(F32)).astype(BF16)

        gather(2 * r + 1)

        def update_slice(s):
            k = s // 2
            rows = pl.ds(pl.multiple_of(lax.rem(s, 2) * 64, 64), 64)
            block = pieces[k]
            return dot(zs[0, rows, :], block) + dot(zs[1, rows, :], block)

        for d in range(1, NT):
            to = lax.rem(me + d, NT)
            sb[r, to, 0:64, :] = update_slice(to).astype(BF16)
            send(sb.at[r, to], rb.at[r, me], tm_s.at[1, r, to], tm_r.at[1, r, me], (sp, to))
        level_send(1, level_sum(0))
        total = update_slice(me)
        frame = sb[r, me, 64:80, :].astype(F32)
        for d in range(1, NT):
            other = lax.rem(me + d, NT)
            arrived(rb.at[r, other], tm_s.at[1, r, other], tm_r.at[1, r, other], (sp, other))
            total = total + rb[r, other, 0:64, :].astype(F32)
            frame = frame + rb[r, other, 64:80, :].astype(F32)
        my_k = me // 2
        my_rows = pl.ds(pl.multiple_of(lax.rem(me, 2) * 64, 64), 64)
        renewed = jnp.maximum(source[my_k, my_rows, :].astype(F32) + total, 0.0).astype(BF16)
        foot[r, my_k, my_rows, :] = renewed
        my_blocks = pl.ds(pl.multiple_of(me * 8, 8), 8)
        for c in range(2):
            scale = jnp.concatenate([square_time[c]] * (BV // NC), axis=1)
            bgs[r, c, my_blocks, :] = jnp.maximum(
                space[c, my_blocks, :] + frame[c * 8 : (c + 1) * 8] / (2.0 * scale), 0.0
            )
        for d in range(1, NT):
            to = lax.rem(me + d, NT)
            send(foot.at[r, my_k, my_rows], foot.at[r, my_k, my_rows], tm_s.at[2, r, to], tm_r.at[2, r, me], (sp, to))
            send(bgs.at[r, :, my_blocks], bgs.at[r, :, my_blocks], tm_s.at[3, r, to], tm_r.at[3, r, me], (sp, to))
        level_send(2, level_sum(1))
        for d in range(1, NT):
            other = lax.rem(me + d, NT)
            k = other // 2
            rows = pl.ds(pl.multiple_of(lax.rem(other, 2) * 64, 64), 64)
            blocks = pl.ds(pl.multiple_of(other * 8, 8), 8)
            arrived(foot.at[r, k, rows], tm_s.at[2, r, other], tm_r.at[2, r, other], (sp, other))
            arrived(bgs.at[r, :, blocks], tm_s.at[3, r, other], tm_r.at[3, r, other], (sp, other))
        if r + 1 < ROUNDS:
            stage_halo(r + 1, foot.at[r])
            to_neighbours(r + 1, halo_out.at[r + 1], halo_out.at[r + 1], lambda s: halo_f.at[r + 1, s])
        packed = level_sum(2)
        for c in range(2):
            change = packed[:, c : c + 1] / (2.0 * packed[:, 2 + c : 3 + c])
            bts[c] = jnp.maximum(bts[c] + jnp.broadcast_to(change, (FR, NC)), 0.0)

    out_tr[...] = traces_now
    out_f[...] = foot[ROUNDS - 1]
    out_bg[...] = bgs[ROUNDS - 1]
    out_bt[...] = bts[...]
    for copy in sends:
        copy.wait_send()


def solution(mesh):
    nsp = mesh.shape["space"]
    sizes = [2, min(4, nsp // 2), nsp // 2 // min(4, nsp // 2)]
    levels = ((1, sizes[0]), (2, sizes[1]), (2 * sizes[1], sizes[2]))
    vmem = pl.BlockSpec(memory_space=pltpu.VMEM)
    smem = pl.BlockSpec(memory_space=pltpu.SMEM)

    def body(activity, footprints, traces, bg_space, bg_time, block_lists, group_order):
        f0 = footprints[0].reshape(NC, BPG, BV).transpose(1, 0, 2)
        tr0 = traces[0].reshape(NC, FR).T
        bt0 = jnp.broadcast_to(bg_time[:, :, None], (2, FR, NC))
        out_tr, out_f, out_bg, out_bt = pl.pallas_call(
            functools.partial(kernel, nsp, levels),
            out_shape=(
                jax.ShapeDtypeStruct((FR, NC), F32),
                jax.ShapeDtypeStruct((BPG, NC, BV), BF16),
                jax.ShapeDtypeStruct((2, VB, BV), F32),
                jax.ShapeDtypeStruct((2, FR, NC), F32),
            ),
            in_specs=[vmem] * 5 + [smem] * 2,
            out_specs=(vmem,) * 4,
            scratch_shapes=[
                pltpu.VMEM((FR, BPG * NC), jnp.int32),
                pltpu.VMEM((2 * ROUNDS, EXT, FR, BV), BF16),
                pltpu.VMEM((BPG, NG * FR, BV), BF16),
                pltpu.VMEM((ROUNDS, BPG, NC, BV), BF16),
                pltpu.VMEM((ROUNDS, 2, VB, BV), F32),
                pltpu.VMEM((2, FR, NC), F32),
                pltpu.VMEM((ROUNDS, 2, NC, BV), BF16),
                pltpu.VMEM((ROUNDS, NC, BV), BF16),
                pltpu.VMEM((ROUNDS + 1, 2, FR + G, NC), BF16),
                pltpu.VMEM((ROUNDS + 1, FR + G, NC), BF16),
                pltpu.VMEM((ROUNDS, G + 8, NC), F32),
                pltpu.VMEM((ROUNDS, NT, G + 8, NC), F32),
                pltpu.VMEM((ROUNDS, NT, 80, BV), BF16),
                pltpu.VMEM((ROUNDS, NT, 80, BV), BF16),
                pltpu.VMEM((8 * FR, 48), F32),
                pltpu.VMEM((ROUNDS, 3, 4, FR, NC), F32),
                pltpu.VMEM((8, NC), F32),
                pltpu.VMEM((2, NC, NG * FR), BF16),
                pltpu.VMEM((48, 8 * FR), BF16),
                pltpu.SemaphoreType.DMA((9, 2)),
                pltpu.SemaphoreType.DMA((9, 2)),
                pltpu.SemaphoreType.DMA((4, ROUNDS, NT)),
                pltpu.SemaphoreType.DMA((4, ROUNDS, NT)),
                pltpu.SemaphoreType.DMA((ROUNDS, 3, 4)),
                pltpu.SemaphoreType.DMA((ROUNDS, 3, 4)),
            ],
            compiler_params=pltpu.CompilerParams(
                collective_id=0, has_side_effects=True, vmem_limit_bytes=48 * 1024 * 1024
            ),
        )(activity, f0, tr0, bg_space, bt0, block_lists[0], group_order[0])
        return (
            out_tr.T.reshape(1, NG, G, FR),
            out_f.transpose(1, 0, 2).reshape(1, NG, G, BPG, BV),
            out_bg,
            out_bt[:, :, 0],
        )

    return jax.shard_map(
        body,
        mesh=mesh,
        in_specs=(
            P("space", "tm", None),
            P("space", None, None, None, None),
            P("space", None, None, "tm"),
            P(None, "space", None),
            P(None, "tm"),
            P("space", None, None),
            P("space", None),
        ),
        out_specs=(
            P("space", None, None, "tm"),
            P("space", None, None, None, None),
            P(None, "space", None),
            P(None, "tm"),
        ),
        check_vma=False,
    )
```

time: 649 us -> 117 us (0.18); the launches traced: 641 us -> 117 us
  blocking collectives: 224 us -> 0 us
  other arithmetic: 126 us -> 0 us
  Pallas kernels: 0 us -> 106 us
  local copies, waits for them, and re-layouts: 80.4 us -> 10 us
  matrix products: 66 us -> 0 us
  waiting for transfers between devices: 65 us -> 0 us
  starting transfers between devices: 47.7 us -> 0 us
  between operations: 31.4 us -> 0.66 us
    psum x4 -> x0, blocking collectives: 224 us -> none  [the longest x2 161 us: body(): lax.psum((voxel_part, squares_space_part), 'space')]
    pallas_call x0 -> x1, Pallas kernels: none -> 106 us  [body(): pl.pallas_call(functools.partial(kernel, nsp, levels), out_shape=(jax.Sha...]
    another operation x24 -> x0, other arithmetic: 95.1 us -> none  [the longest x13 51 us: group_inverse(): lower_factor = jnp.linalg.cholesky(matrices)]
    dot_general x60 -> x0, matrix products: 64.5 us -> none  [the longest x16 12.3 us: temporal(): jnp.dot(inverse[chosen], remain, precision=lax.Precision.HIGHEST)]
    psum x2 -> x0, waiting for transfers between devices: 58.4 us -> none  [body(): lax.psum((project, correlation, frame_part, squares_time_part), 'tm')]
    ppermute x16 -> x0, starting transfers between devices: 47.4 us -> none  [the longest x8 35.4 us: with_halo(): lax.ppermute(lax.slice_in_dim(block, block.shape[dim] - width, None, axis...]
    unnamed x149 -> x9, local copies, waits for them, and re-layouts: 31.3 us -> 6.24 us
    gather x8 -> x0, local copies, waits for them, and re-layouts: 16 us -> none  [the longest x4 12.4 us: pieces_of(): jnp.take(extended_res, block_row.reshape(-1), axis=0)]
  transfers between devices with their start and end apart: 18 -> 0, of which waited for: 5 -> 0; matrix products, arithmetic and copies ran while one was open for 20% -> 0% of each run, Pallas kernels for 0% -> 0%
where the time goes in v1:
time: 117 us
  Pallas kernels  106 us (91%)
  local copies, waits for them, and re-layouts  10 us (9%)
    pallas_call x1, Pallas kernels, body(): pl.pallas_call(functools.partial(kernel, nsp, levels), out_shape=(jax.Sha...  106 us
    unnamed x9, local copies, waits for them, and re-layouts  6.24 us

profile of v1, /device:TPU:6, one launch (start us, length us, event | category | flops | bytes accessed | tf_op | source)
XLA Modules:
  0.0 116.6 jit_solution(143105055606013594)
XLA Ops:
  0.6 0.8 copy.18.bl
  1.4 0.9 copy.17
  2.3 0.8 broadcast_in_dim.2.bt0
  3.1 1.1 copy.16
  4.2 0.0 copy-start
  4.2 1.6 %copy-done = bf16[64,32,512]{2,1,0:T(8,128)(2,1)S(1)} copy-done((bf16[64,32,512]{2,1,0:T(8,128)(2,1)S(1)}, bf16[64,32,512]{2,1,0:T(8,128)(2,1)}, u32[]{:S(2)}) %copy-start) | copy-done | bytes 2097176
  5.8 0.0 copy-start.1
  5.8 0.9 copy-done.1
  6.8 0.0 copy-start.2
  6.8 0.7 copy-done.2
  7.4 105.9 %shard_map.102 = (f32[32,128]{1,0:T(8,128)S(1)}, bf16[4,128,512]{2,1,0:T(8,128)(2,1)S(1)}, f32[2,64,512]{2,1,0:T(8,128)S(1)}, f32[2,32,128]{2,1,0:T(8,128)S(1)}) custom-call(bf16[64,32,512]{2,1,0:T(8,128)(2,1)S(1)} %copy-done, bf16[4,128,512]{2,1,0:T(8,128)(2,1)S(1)} %bitcast.12, f32[32,128]{1,0:T(8,128)S(1)} %bitcast.14, f32[2,64,512]{2,1,0:T(8,128)S(1)} %copy-done.1, ...), custom_call_target="tpu_custom_call" | custom-call | tf_op jit(solution)/shard_map/pallas_call | solution.py:423
  113.4 1.2 %copy.20 = bf16[1,8,16,4,512]{4,3,2,1,0:T(4,128)(2,1)} copy(bf16[1,8,16,4,512]{4,2,1,3,0:T(8,128)(2,1)S(1)} %bitcast.13) | data formatting | bytes 1048576
  114.6 0.7 slice_reduce_fusion
  115.2 0.7 copy.19
  115.9 0.7 copy.22
Async XLA Ops:
  4.2 1.6 %copy-start = (bf16[64,32,512]{2,1,0:T(8,128)(2,1)S(1)}, bf16[64,32,512]{2,1,0:T(8,128)(2,1)}, u32[]{:S(2)}) copy-start(bf16[64,32,512]{2,1,0:T(8,128)(2,1)} %act.1) | copy-start | bytes 6291460
  5.8 0.9 copy-start.1
  6.8 0.7 copy-start.2
